TPU v7x, 128 devices: a whole 4x4x4 slice. The times are simulated.
128 devices in a mesh: au: 16 (over x, y), vert: 8 (over z, core).
Axes of the slice: x: 4, y: 4, z: 4, core: 2. Of those that a mesh axis runs over, the one named last changes fastest.
Arguments:
- visibility: bfloat16 [262144, 128], P(('au', 'vert')), may hold values from -6 to 6
- destination: int32 [262144, 1], P(('au', 'vert')), may hold values from 0 to 127; in each aligned block of 2048 rows (0 to 2047, 2048 to 4095, ...) at most 32 rows name the same one
- cell_u: int32 [262144], P(('au', 'vert')), may hold values from 0 to 127
- cell_v: int32 [262144], P(('au', 'vert')), may hold values from 0 to 127
- tap_u: int32 [262144], P(('au', 'vert')), may hold values from 0 to 127
- tap_v: int32 [262144], P(('au', 'vert')), may hold values from 0 to 127
- kernel_table: bfloat16 [128, 8], replicated, may hold values from 0.19921875 to 1
Outputs:
- uv_grid: float32 [2048, 1024, 128], P('au', 'vert')
Inputs may be any that keep to these rules, and one draw needn't show every extreme that they name: `destination`: of the 2048 rows of one device, at most 32 name the same tile, and in every draw some device sends exactly 32 rows to some tile.
All inputs are finite; a program needn't handle non-finite values.
Results may differ from a plain program's by a relative error of at most 0.0029.
Values may be sent and summed in bfloat16 or wider, within the bound.
No kernel may reach another device: no remote copies, remote signals or barrier semaphores. Data moves between devices by JAX's collectives and lax.ppermute only.
A program may use at most 128 MiB of HBM per device.

v0:
```python
import jax
import jax.numpy as jnp
from jax import lax
from jax.experimental import pallas as pl
from jax.experimental.pallas import tpu as pltpu
from jax.sharding import PartitionSpec as P

FEAT = 128
TAPS = 8
TU = 128
TV = 128
CAP = 32
SENT = CAP + 8
BLK = 256
EU = 144
EV = 160
PAD = 4
GROUP = 20
MIB = 1024 * 1024
NT = (((1,), (1,)), ((), ()))

f32 = jnp.float32
bf16 = jnp.bfloat16
i32 = jnp.int32


def iota(shape, dim):
    return lax.broadcasted_iota(i32, shape, dim)


def dot(a, b):
    return jnp.dot(a, b, preferred_element_type=f32)


def earlier(n):
    return (iota((n, n), 0) < iota((n, n), 1)).astype(f32).astype(bf16)


def pack_kernel(
    dest_hbm, cu_hbm, cv_hbm, tu_hbm, tv_hbm, vis_hbm, out_ref,
    dest_ref, cu_ref, cv_ref, tu_ref, tv_ref, vis_ref, slot_v, slot_s, xf, packed, meta, sems,
):
    rows = vis_ref.shape[0]
    ins = [
        pltpu.make_async_copy(there, here, sems.at[i])
        for i, (there, here) in enumerate((
            (dest_hbm, dest_ref), (cu_hbm, cu_ref), (cv_hbm, cv_ref),
            (tu_hbm, tu_ref), (tv_hbm, tv_ref), (vis_hbm, vis_ref),
        ))
    ]
    for copy in ins:
        copy.start()
    tiles = out_ref.shape[0]
    blocks = rows // BLK
    before = earlier(BLK)
    base = jnp.zeros((tiles, 1), f32)
    placed = jnp.zeros((tiles, 4 * CAP), f32)

    @pl.loop(0, tiles)
    def _(t):
        packed[pl.ds(t * CAP, CAP), :] = jnp.zeros((CAP, FEAT), f32)

    for copy in ins[:5]:
        copy.wait()
    tile_ids = iota((tiles, BLK), 0)
    cap_ids = iota((CAP, BLK), 0)
    for b in range(blocks):
        part = pl.ds(b * BLK, BLK)
        d = dest_ref[:, part]
        mine = (tile_ids == d).astype(f32)
        mine16 = mine.astype(bf16)
        rank = jnp.sum(mine * (dot(mine16, before) + base), 0, keepdims=True).astype(i32)
        base = base + jnp.sum(mine, 1, keepdims=True)
        slot = d * CAP + rank
        slot_v[pl.ds(b, 1), :] = slot[:, :BLK // 2] + (slot[:, BLK // 2:] << 16)
        at = cap_ids == rank
        fields = [
            jnp.where(at, (ref[:, part] + 1).astype(f32), 0.0)
            for ref in (cu_ref, cv_ref, tu_ref, tv_ref)
        ]
        fields = jnp.concatenate(fields, 0).astype(bf16)
        placed = placed + lax.dot_general(mine16, fields, NT, preferred_element_type=f32)
    meta[...] = placed
    copy = pltpu.make_async_copy(slot_v, slot_s, sems.at[6])
    copy.start()
    ins[5].wait()

    @pl.loop(0, rows // 32)
    def _(t):
        xf[t] = vis_ref[pl.ds(t * 32, 32), :].astype(f32)

    copy.wait()
    step = 32

    for b in range(blocks):

        @pl.loop(0, BLK // (2 * step))
        def _(t):
            for j in range(step):
                two = slot_s[b, t * step + j]
                at = b * (BLK // step) + t
                packed[pl.ds(two & 0xFFFF, 1), :] = xf[at, pl.ds(j, 1), :]
                packed[pl.ds(two >> 16, 1), :] = xf[at + BLK // (2 * step), pl.ds(j, 1), :]

    @pl.loop(0, tiles)
    def _(t):
        rows_t = packed[pl.ds(t * CAP, CAP), :]
        meta_t = jnp.broadcast_to(meta[pl.ds(t, 1), :], (SENT - CAP, FEAT))
        out_ref[t] = jnp.concatenate([rows_t, meta_t], 0).astype(bf16)


def pack(visibility, destination, cell_u, cell_v, tap_u, tap_v, tiles):
    rows = visibility.shape[0]
    row = lambda x: x.reshape(1, rows)
    return pl.pallas_call(
        pack_kernel,
        in_specs=[pl.BlockSpec(memory_space=pltpu.HBM)] * 6,
        out_shape=jax.ShapeDtypeStruct((tiles, SENT, FEAT), bf16),
        scratch_shapes=[pltpu.VMEM((1, rows), i32)] * 5 + [
            pltpu.VMEM((rows, FEAT), bf16),
            pltpu.VMEM((rows // BLK, BLK // 2), i32),
            pltpu.SMEM((rows // BLK, BLK // 2), i32),
            pltpu.VMEM((rows // 32, 32, FEAT), f32),
            pltpu.VMEM((tiles * CAP, FEAT), f32),
            pltpu.VMEM((tiles, FEAT), f32),
            pltpu.SemaphoreType.DMA((7,)),
        ],
        compiler_params=pltpu.CompilerParams(vmem_limit_bytes=60 * MIB),
        name="pack_rows",
    )(row(destination), row(cell_u), row(cell_v), row(tap_u), row(tap_v), visibility)


def grid_kernel(
    recv_ref, table_hbm, out_hbm, ve_low, ve_high, ue_ref,
    xf, xm, xs, ms, meta, meta_t, pos_v, pos_s, span_v, span_s,
    wu_a, wu_b, taps_a, taps_b, xt_a, xt_b, wv_a, wv_b, table_ref, grid3, sems, out_sems,
):
    grid = grid3.reshape(EV * EU, FEAT)
    sources = recv_ref.shape[0]
    slots = sources * CAP
    blocks = slots // BLK
    lanes = BLK // sources

    @pl.loop(0, sources)
    def _(s):
        x = recv_ref[s].astype(f32)
        xf[s] = x[:CAP]
        meta[pl.ds(s, 1), :] = x[CAP:CAP + 1]

    table_copy = pltpu.make_async_copy(table_hbm, table_ref, sems.at[2])
    table_copy.start()
    placed = meta[...]
    meta_t[...] = placed.T
    keys = 64

    def key_row(b):
        out = []
        for k in range(b * lanes, (b + 1) * lanes):
            cu1 = meta_t[pl.ds(k, 1), :].astype(i32)
            cv1 = meta_t[pl.ds(CAP + k, 1), :].astype(i32)
            out.append(jnp.where(cu1 > 0, (cv1 - 1) >> 1, keys))
        return jnp.concatenate(out, 1)

    key_ids = iota((128, BLK), 0)
    total = jnp.zeros((128, BLK), f32)
    for b in range(blocks):
        total = total + (key_ids == key_row(b)).astype(f32)
    total = jnp.broadcast_to(jnp.sum(total, 1, keepdims=True), (128, 128))
    below = (iota((128, 128), 1) < iota((128, 128), 0)).astype(f32).astype(bf16)
    high = jnp.floor(total * (1.0 / 64.0))
    low = total - 64.0 * high
    start = 64.0 * dot(below, high.astype(bf16)) + dot(below, low.astype(bf16))
    count = start[keys:keys + 1, :]
    lane = iota((128, 128), 1).astype(f32) * BLK
    real = iota((128, 128), 0) < keys
    first = jnp.sum(jnp.where(real & (start + total <= lane), 1.0, 0.0), 0, keepdims=True)
    last = jnp.sum(jnp.where(real & (start < jnp.minimum(lane + BLK, count)), 1.0, 0.0), 0, keepdims=True) - 1.0
    span_v[...] = jnp.concatenate([first, last, count, jnp.zeros((5, 128), f32)], 0).astype(i32)
    span_copy = pltpu.make_async_copy(span_v, span_s, sems.at[0])
    span_copy.start()
    before = earlier(BLK)
    base = start[:, 0:1]
    for b in range(blocks):
        mine = (key_ids == key_row(b)).astype(f32)
        pos = jnp.sum(mine * (dot(mine.astype(bf16), before) + base), 0, keepdims=True)
        pos = pos.astype(i32)
        pos_v[pl.ds(b, 1), :] = pos[:, :BLK // 2] + (pos[:, BLK // 2:] << 16)
        base = base + jnp.sum(mine, 1, keepdims=True)
    pos_copy = pltpu.make_async_copy(pos_v, pos_s, sems.at[1])
    pos_copy.start()
    for k in range(CAP):
        xm[pl.ds(k * sources, sources), :] = pltpu.roll(placed, (FEAT - k) % FEAT, 1)

    @pl.loop(0, EV)
    def _(t):
        grid[pl.ds(t * EU, EU), :] = jnp.zeros((EU, FEAT), f32)

    table_copy.wait()
    pos_copy.wait()
    span_copy.wait()

    @pl.loop(0, sources)
    def _(s):
        for b in range(blocks):
            two = pos_s[b, s]
            for k, p in ((2 * b, two & 0xFFFF), (2 * b + 1, two >> 16)):
                xs[pl.ds(p, 1), :] = xf[s, pl.ds(k, 1), :]
                ms[pl.ds(p, 1), :] = xm[pl.ds(k * sources + s, 1), :]

    table_tr = table_ref[...]
    pick = (iota((8, FEAT), 1) == CAP * iota((8, FEAT), 0)).astype(f32).astype(bf16)
    phase_ids = iota((128, BLK), 0)
    u_ids = iota((EU, BLK), 0)
    t_ids = iota((GROUP + 4, BLK), 0)
    chunks = (span_s[2, 0] + BLK - 1) // BLK
    sets = ((wu_a, taps_a, xt_a, wv_a), (wu_b, taps_b, xt_b, wv_b))

    def v_weights(taps, v_at):
        off = (t_ids + v_at) - taps[8:9].astype(i32)
        wv = jnp.zeros((GROUP + 4, BLK), f32)
        for a in range(TAPS):
            wv = jnp.where(off == a, taps[a:a + 1], wv)
        return wv.astype(bf16)

    def prepare(c, into):
        wu, taps, xt, wv = into
        part = pl.ds(c * BLK, BLK)
        xt[...] = xs[part, :].T.astype(bf16)
        fields = lax.dot_general(pick, ms[part, :].astype(bf16), NT, preferred_element_type=f32).astype(i32) - 1
        cu, cv, tu, tv = (fields[i:i + 1] for i in range(4))
        ku = dot(table_tr, (phase_ids == tu).astype(f32).astype(bf16))
        kv = dot(table_tr, (phase_ids == tv).astype(f32).astype(bf16))
        off = u_ids - (cu + 4)
        weights = jnp.zeros((EU, BLK), f32)
        for a in range(TAPS):
            weights = jnp.where(off == a, ku[a:a + 1], weights)
        wu[...] = weights.astype(bf16)
        all_taps = jnp.concatenate([kv, jnp.broadcast_to(cv, (8, BLK)).astype(f32)], 0)
        taps[...] = all_taps
        wv[...] = v_weights(all_taps, 2 * span_s[0, c])

    def add_cells(v_at, wu, xt, wv):
        for j in range(0, GROUP, 2):
            rhs = jnp.concatenate([xt[...] * wv[i:i + 1] for i in (j, j + 1)], 0)
            add = lax.dot_general(wu[...], rhs, NT, preferred_element_type=f32)
            for i in range(2):
                at = pl.ds((v_at + j + i) * EU, EU)
                grid[at, :] = grid[at, :] + add[:, i * FEAT:(i + 1) * FEAT]

    prepare(0, sets[0])

    @pl.loop(0, (chunks + 1) // 2)
    def _(pair):
        for half in range(2):
            c = 2 * pair + half
            wu, taps, xt, wv = sets[half]
            v_first = 2 * span_s[0, c]
            steps = 2 * (span_s[1, c] - span_s[0, c]) + TAPS + 1
            prepare(jnp.minimum(c + 1, slots // BLK - 1), sets[1 - half])
            add_cells(v_first, wu, xt, wv[...])

            @pl.loop(1, (steps + GROUP - 1) // GROUP)
            def _(g):
                v_at = v_first + g * GROUP
                add_cells(v_at, wu, xt, v_weights(taps[...], v_at))

    def out_copy(u):
        return pltpu.make_async_copy(grid3.at[pl.ds(PAD, TV), 8 + u], out_hbm.at[u], out_sems.at[0])

    @pl.loop(0, TU)
    def _(u):
        out_copy(u).start()

    ve_low[...] = grid[pl.ds(0, PAD * EU), :].astype(bf16)
    ve_high[...] = grid[pl.ds((TV + PAD) * EU, PAD * EU), :].astype(bf16)

    def edge_copy(e, u):
        at = (PAD, TU + 8)[e] + u
        return pltpu.make_async_copy(grid3.at[pl.ds(PAD, TV), at], ue_ref.at[e, u], out_sems.at[1])

    for e in range(2):
        for u in range(PAD):
            edge_copy(e, u).start()
    for e in range(2):
        for u in range(PAD):
            edge_copy(e, u).wait()

    @pl.loop(0, TU)
    def _(u):
        out_copy(u).wait()


def grid_rows(recv, table):
    sources = recv.shape[0]
    slots = sources * CAP
    vmem = pl.BlockSpec(memory_space=pltpu.VMEM)
    return pl.pallas_call(
        grid_kernel,
        in_specs=[vmem, pl.BlockSpec(memory_space=pltpu.HBM)],
        out_specs=(pl.BlockSpec(memory_space=pltpu.HBM), vmem, vmem, vmem),
        out_shape=(
            jax.ShapeDtypeStruct((TU, TV, FEAT), f32),
            jax.ShapeDtypeStruct((PAD * EU, FEAT), bf16),
            jax.ShapeDtypeStruct((PAD * EU, FEAT), bf16),
            jax.ShapeDtypeStruct((2, PAD, TV, FEAT), f32),
        ),
        scratch_shapes=[
            pltpu.VMEM((sources, CAP, FEAT), f32),
            pltpu.VMEM((slots, FEAT), f32),
            pltpu.VMEM((slots, FEAT), f32),
            pltpu.VMEM((slots, FEAT), f32),
            pltpu.VMEM((sources, FEAT), f32),
            pltpu.VMEM((FEAT, sources), f32),
            pltpu.VMEM((slots // BLK, BLK // 2), i32),
            pltpu.SMEM((slots // BLK, BLK // 2), i32),
            pltpu.VMEM((8, 128), i32),
            pltpu.SMEM((8, 128), i32),
            pltpu.VMEM((EU, BLK), bf16),
            pltpu.VMEM((EU, BLK), bf16),
            pltpu.VMEM((16, BLK), f32),
            pltpu.VMEM((16, BLK), f32),
            pltpu.VMEM((FEAT, BLK), bf16),
            pltpu.VMEM((FEAT, BLK), bf16),
            pltpu.VMEM((GROUP + 4, BLK), bf16),
            pltpu.VMEM((GROUP + 4, BLK), bf16),
            pltpu.VMEM((TAPS, 128), bf16),
            pltpu.VMEM((EV, EU, FEAT), f32),
            pltpu.SemaphoreType.DMA((3,)),
            pltpu.SemaphoreType.DMA((2,)),
        ],
        compiler_params=pltpu.CompilerParams(vmem_limit_bytes=48 * MIB),
        name="grid_rows",
    )(recv, table)


def corner_kernel(low_ref, high_ref, ue_ref, send_low, send_high, low, high, edges):
    edges[...] = ue_ref[...]
    low[...] = low_ref[...].astype(f32)
    high[...] = high_ref[...].astype(f32)
    for e, (at, send) in enumerate(((PAD, send_low), (TU + 8, send_high))):
        for u in range(PAD):
            there = pl.ds(at + u, PAD, stride=EU)
            edges[e, u, 0:PAD, :] += low[there, :]
            edges[e, u, TV - PAD:TV, :] += high[there, :]
        send[...] = edges[e].astype(bf16)


def add_corners(low, high, ue):
    edge = jax.ShapeDtypeStruct(ue.shape[1:], bf16)
    return pl.pallas_call(
        corner_kernel,
        out_shape=(edge, edge),
        scratch_shapes=[
            pltpu.VMEM(low.shape, f32),
            pltpu.VMEM(high.shape, f32),
            pltpu.VMEM(ue.shape, f32),
        ],
        compiler_params=pltpu.CompilerParams(vmem_limit_bytes=8 * MIB),
        name="add_corners",
    )(low, high, ue)


def v_edge_kernel(out_in, low_ref, high_ref, out_hbm, own_ref, low, high, edges, sems):
    def copy(e, back):
        there = out_hbm.at[:, pl.ds(e * (TV - 8), 8)]
        ends = (edges.at[e], there) if back else (there, edges.at[e])
        return pltpu.make_async_copy(*ends, sems.at[e])

    copy(0, False).start()
    copy(1, False).start()
    low[...] = low_ref[...].astype(f32)
    high[...] = high_ref[...].astype(f32)
    for e, (halo, at) in enumerate(((low, 0), (high, 8 - PAD))):
        copy(e, False).wait()

        @pl.loop(0, TU // 8)
        def _(t):
            for j in range(8):
                u = t * 8 + j
                edges[e, u, at:at + PAD, :] += halo[pl.ds(8 + u, PAD, stride=EU), :]

        copy(e, True).start()
    copy(0, True).wait()
    copy(1, True).wait()
    own = [
        pltpu.make_async_copy(out_hbm.at[pl.ds(e * (TU - PAD), PAD)], own_ref.at[e], sems.at[e])
        for e in range(2)
    ]
    own[0].start()
    own[1].start()
    own[0].wait()
    own[1].wait()


def add_v_edges(out, low, high):
    vmem = pl.BlockSpec(memory_space=pltpu.VMEM)
    hbm = pl.BlockSpec(memory_space=pl.ANY)
    return pl.pallas_call(
        v_edge_kernel,
        in_specs=[hbm, vmem, vmem],
        out_specs=(hbm, vmem),
        out_shape=(
            jax.ShapeDtypeStruct(out.shape, f32),
            jax.ShapeDtypeStruct((2, PAD, TV, FEAT), f32),
        ),
        scratch_shapes=[
            pltpu.VMEM(low.shape, f32),
            pltpu.VMEM(high.shape, f32),
            pltpu.VMEM((2, TU, 8, FEAT), f32),
            pltpu.SemaphoreType.DMA((2,)),
        ],
        input_output_aliases={0: 0},
        compiler_params=pltpu.CompilerParams(vmem_limit_bytes=8 * MIB),
        name="add_v_edges",
    )(out, low, high)


def u_edge_kernel(out_in, low_ref, high_ref, own_ref, out_hbm, edges, sems):
    def copy(e):
        return pltpu.make_async_copy(edges.at[e], out_hbm.at[pl.ds(e * (TU - PAD), PAD)], sems.at[e])

    edges[0] = own_ref[0] + low_ref[...].astype(f32)
    copy(0).start()
    edges[1] = own_ref[1] + high_ref[...].astype(f32)
    copy(1).start()
    copy(0).wait()
    copy(1).wait()


def add_u_edges(out, low, high, own):
    vmem = pl.BlockSpec(memory_space=pltpu.VMEM)
    hbm = pl.BlockSpec(memory_space=pl.ANY)
    return pl.pallas_call(
        u_edge_kernel,
        in_specs=[hbm, vmem, vmem, vmem],
        out_specs=hbm,
        out_shape=jax.ShapeDtypeStruct(out.shape, f32),
        scratch_shapes=[pltpu.VMEM(own.shape, f32), pltpu.SemaphoreType.DMA((2,))],
        input_output_aliases={0: 0},
        compiler_params=pltpu.CompilerParams(vmem_limit_bytes=8 * MIB),
        name="add_u_edges",
    )(out, low, high, own)


def shifted(x, axis, up):
    n = lax.axis_size(axis)
    pairs = [(i, i + 1) if up else (i + 1, i) for i in range(n - 1)]
    return lax.ppermute(x, axis, pairs)


def local(visibility, destination, cell_u, cell_v, tap_u, tap_v, kernel_table):
    axes = ("au", "vert")
    tiles = lax.axis_size("au") * lax.axis_size("vert")
    sent = pack(visibility, destination, cell_u, cell_v, tap_u, tap_v, tiles)
    recv = lax.all_to_all(sent, axes, split_axis=0, concat_axis=0, tiled=True)
    out, ve_low, ve_high, ue = grid_rows(recv, kernel_table.T)
    v_low = shifted(ve_high, "vert", True)
    v_high = shifted(ve_low, "vert", False)
    send_low, send_high = add_corners(v_low, v_high, ue)
    u_low = shifted(send_high, "au", True)
    u_high = shifted(send_low, "au", False)
    out, own = add_v_edges(out, v_low, v_high)
    return add_u_edges(out, u_low, u_high, own)


def solution(mesh):
    rows = P(("au", "vert"))
    return jax.shard_map(
        local,
        mesh=mesh,
        in_specs=(P(("au", "vert"), None), P(("au", "vert"), None), rows, rows, rows, rows, P()),
        out_specs=P("au", "vert", None),
        check_vma=False,
    )
```

profile of v0, /device:TPU:1, one launch (start us, length us, event | category | flops | bytes accessed | tf_op | source)
XLA Modules:
  0.0 86.2 jit_solution(15097053042794360268)
XLA Ops:
  0.0 6.8 %pack_rows.1 = bf16[128,40,128]{2,1,0:T(8,128)(2,1)} custom-call(s32[1,2048]{1,0:T(1,128)} %bitcast.7, s32[1,2048]{1,0:T(1,128)} %bitcast.8, s32[1,2048]{1,0:T(1,128)} %bitcast.9, s32[1,2048]{1,0:T(1,128)} %bitcast.10, s32[1,2048]{1,0:T(1,128)} %bitcast.11, bf16[2048,128]{1,0:T(8,128)(2,1)} %vis_hbm.1), custom_call_target="tpu_custom_call" | custom-call | tf_op jit(solution)/shard_map/pack_rows/pallas_call | solution.py:115
  6.8 33.6 %all_to_all.5.recv_ref = bf16[128,40,128]{2,1,0:T(8,128)(2,1)S(1)} all-to-all(bf16[128,40,128]{2,1,0:T(8,128)(2,1)} %pack_rows.1), channel_id=1, replica_groups=mesh['au'=16,'vert'=8] {'au','vert'}, dimensions={0} | all-to-all | bytes 2621440 | tf_op jit(solution)/shard_map/all_to_all | solution.py:455
  40.4 0.0 copy-start
  40.4 0.7 copy-done
  41.1 26.1 %grid_rows.1 = (f32[128,128,128]{2,1,0:T(8,128)}, bf16[576,128]{1,0:T(8,128)(2,1)S(1)}, bf16[576,128]{1,0:T(8,128)(2,1)S(1)}, f32[2,4,128,128]{3,2,1,0:T(8,128)S(1)}) custom-call(bf16[128,40,128]{2,1,0:T(8,128)(2,1)S(1)} %all_to_all.5.recv_ref, bf16[8,128]{1,0:T(8,128)(2,1)S(1)} %bitcast.6), custom_call_target="tpu_custom_call" | custom-call | tf_op jit(solution)/shard_map/grid_rows/pallas_call | solution.py:297
  67.3 4.5 %collective-permute-start = (bf16[576,128]{1,0:T(8,128)(2,1)S(1)}, bf16[576,128]{1,0:T(8,128)(2,1)S(1)}, u32[]{:S(2)}, u32[]{:S(2)}) collective-permute-start(bf16[576,128]{1,0:T(8,128)(2,1)S(1)} %get-tuple-element.14), channel_id=1, source_target_pairs={{0,1},{1,2},{2,3},{3,4},{4,5},{5,6},{6,7},{8,9},{9,10},{10,11},{11... | collective-permute-start | bytes 442376 | tf_op jit(solution)/shard_map/ppermute | solution.py:448
  71.8 1.9 %collective-permute-start.1 = (bf16[576,128]{1,0:T(8,128)(2,1)S(1)}, bf16[576,128]{1,0:T(8,128)(2,1)S(1)}, u32[]{:S(2)}, u32[]{:S(2)}) collective-permute-start(bf16[576,128]{1,0:T(8,128)(2,1)S(1)} %get-tuple-element.15), channel_id=1, source_target_pairs={{1,0},{2,1},{3,2},{4,3},{5,4},{6,5},{7,6},{9,8},{10,9},{11,10},{12... | collective-permute-start | bytes 442376 | tf_op jit(solution)/shard_map/ppermute | solution.py:448
  73.7 0.2 collective-permute-done.low_ref
  73.9 4.4 %collective-permute-done.1.high_ref = bf16[576,128]{1,0:T(8,128)(2,1)S(1)} collective-permute-done((bf16[576,128]{1,0:T(8,128)(2,1)S(1)}, bf16[576,128]{1,0:T(8,128)(2,1)S(1)}, u32[]{:S(2)}, u32[]{:S(2)}) %collective-permute-start.1) | collective-permute-done | bytes 147488 | tf_op jit(solution)/shard_map/ppermute | solution.py:448
  78.3 0.1 add_corners.1
  78.4 1.3 %collective-permute-start.2 = (bf16[4,128,128]{2,1,0:T(8,128)(2,1)S(1)}, bf16[4,128,128]{2,1,0:T(8,128)(2,1)S(1)}, u32[]{:S(2)}, u32[]{:S(2)}) collective-permute-start(bf16[4,128,128]{2,1,0:T(8,128)(2,1)S(1)} %get-tuple-element.18), channel_id=1, source_target_pairs={{0,8},{8,16},{16,24},{24,32},{32,40},{40,48},{48,56},{56,64},{64,7... | collective-permute-start | bytes 393224 | tf_op jit(solution)/shard_map/ppermute | solution.py:448
  79.7 1.3 %collective-permute-start.3 = (bf16[4,128,128]{2,1,0:T(8,128)(2,1)S(1)}, bf16[4,128,128]{2,1,0:T(8,128)(2,1)S(1)}, u32[]{:S(2)}, u32[]{:S(2)}) collective-permute-start(bf16[4,128,128]{2,1,0:T(8,128)(2,1)S(1)} %get-tuple-element.19), channel_id=1, source_target_pairs={{8,0},{16,8},{24,16},{32,24},{40,32},{48,40},{56,48},{64,56},{72,6... | collective-permute-start | bytes 393224 | tf_op jit(solution)/shard_map/ppermute | solution.py:448
  81.0 3.2 %add_v_edges.1 = (f32[128,128,128]{2,1,0:T(8,128)}, f32[2,4,128,128]{3,2,1,0:T(8,128)S(1)}) custom-call(f32[128,128,128]{2,1,0:T(8,128)} %get-tuple-element.13.out_in, bf16[576,128]{1,0:T(8,128)(2,1)S(1)} %collective-permute-done.low_ref, bf16[576,128]{1,0:T(8,128)(2,1)S(1)} %collective-permute-done.1.high_ref), custom_call_target="tpu_custom_call", output_to_operand_aliasing={{0}: (0, {})} | custom-call | tf_op jit(solution)/shard_map/add_v_edges/pallas_call | solution.py:398
  84.2 0.0 collective-permute-done.2.low_ref
  84.2 1.2 %collective-permute-done.3.high_ref = bf16[4,128,128]{2,1,0:T(8,128)(2,1)S(1)} collective-permute-done((bf16[4,128,128]{2,1,0:T(8,128)(2,1)S(1)}, bf16[4,128,128]{2,1,0:T(8,128)(2,1)S(1)}, u32[]{:S(2)}, u32[]{:S(2)}) %collective-permute-start.3) | collective-permute-done | bytes 131104 | tf_op jit(solution)/shard_map/ppermute | solution.py:448
  85.4 0.8 add_u_edges.1
Async XLA Ops:
  40.4 0.7 copy-start
  67.3 6.6 %collective-permute-start = (bf16[576,128]{1,0:T(8,128)(2,1)S(1)}, bf16[576,128]{1,0:T(8,128)(2,1)S(1)}, u32[]{:S(2)}, u32[]{:S(2)}) collective-permute-start(bf16[576,128]{1,0:T(8,128)(2,1)S(1)} %get-tuple-element.14), channel_id=1, source_target_pairs={{0,1},{1,2},{2,3},{3,4},{4,5},{5,6},{6,7},{8,9},{9,10},{10,11},{11... | collective-permute-start | bytes 442376 | tf_op jit(solution)/shard_map/ppermute | solution.py:448
  71.8 6.5 %collective-permute-start.1 = (bf16[576,128]{1,0:T(8,128)(2,1)S(1)}, bf16[576,128]{1,0:T(8,128)(2,1)S(1)}, u32[]{:S(2)}, u32[]{:S(2)}) collective-permute-start(bf16[576,128]{1,0:T(8,128)(2,1)S(1)} %get-tuple-element.15), channel_id=1, source_target_pairs={{1,0},{2,1},{3,2},{4,3},{5,4},{6,5},{7,6},{9,8},{10,9},{11,10},{12... | collective-permute-start | bytes 442376 | tf_op jit(solution)/shard_map/ppermute | solution.py:448
  78.4 5.9 %collective-permute-start.2 = (bf16[4,128,128]{2,1,0:T(8,128)(2,1)S(1)}, bf16[4,128,128]{2,1,0:T(8,128)(2,1)S(1)}, u32[]{:S(2)}, u32[]{:S(2)}) collective-permute-start(bf16[4,128,128]{2,1,0:T(8,128)(2,1)S(1)} %get-tuple-element.18), channel_id=1, source_target_pairs={{0,8},{8,16},{16,24},{24,32},{32,40},{40,48},{48,56},{56,64},{64,7... | collective-permute-start | bytes 393224 | tf_op jit(solution)/shard_map/ppermute | solution.py:448
  79.7 5.7 %collective-permute-start.3 = (bf16[4,128,128]{2,1,0:T(8,128)(2,1)S(1)}, bf16[4,128,128]{2,1,0:T(8,128)(2,1)S(1)}, u32[]{:S(2)}, u32[]{:S(2)}) collective-permute-start(bf16[4,128,128]{2,1,0:T(8,128)(2,1)S(1)} %get-tuple-element.19), channel_id=1, source_target_pairs={{8,0},{16,8},{24,16},{32,24},{40,32},{48,40},{56,48},{64,56},{72,6... | collective-permute-start | bytes 393224 | tf_op jit(solution)/shard_map/ppermute | solution.py:448
where the time goes:
time: 86.3 us; the launch traced here: 86.2 us
  Pallas kernels  37.1 us (43%)
  blocking collectives  33.6 us (39%)
  starting transfers between devices  9.04 us (10%)
  waiting for transfers between devices  5.69 us (7%)
    all_to_all x1, blocking collectives, local(): recv = lax.all_to_all(sent, axes, split_axis=0, concat_axis=0, tiled=True)  33.6 us
    pallas_call x1, Pallas kernels, grid_rows(): pl.pallas_call(grid_kernel, in_specs=[vmem, pl.BlockSpec(memory_space=plt...  26.1 us
    ppermute x4, starting transfers between devices, shifted(): return lax.ppermute(x, axis, pairs)  9.04 us
    pallas_call x1, Pallas kernels, pack(): pl.pallas_call(pack_kernel, in_specs=[pl.BlockSpec(memory_space=pltpu.HBM...  6.83 us
    ppermute x4, waiting for transfers between devices, shifted(): return lax.ppermute(x, axis, pairs)  5.69 us
    pallas_call x1, Pallas kernels, add_v_edges(): pl.pallas_call(v_edge_kernel, in_specs=[hbm, vmem, vmem], out_specs=(hbm,...  3.24 us
  transfers between devices with their start and end apart: 4, of which 3 were waited for; matrix products, arithmetic and copies ran while one was open for 0% of the time, Pallas kernels for 4%

commit v1 on v0

--- a/solution.py
+++ b/solution.py
@@ -56,9 +56,9 @@
     base = jnp.zeros((tiles, 1), f32)
     placed = jnp.zeros((tiles, 4 * CAP), f32)
 
-    @pl.loop(0, tiles)
+    @pl.loop(0, tiles // 4)
     def _(t):
-        packed[pl.ds(t * CAP, CAP), :] = jnp.zeros((CAP, FEAT), f32)
+        packed[pl.ds(t * 4 * CAP, 4 * CAP), :] = jnp.zeros((4 * CAP, FEAT), f32)
 
     for copy in ins[:5]:
         copy.wait()
@@ -85,9 +85,10 @@
     copy.start()
     ins[5].wait()
 
-    @pl.loop(0, rows // 32)
+    @pl.loop(0, rows // 128)
     def _(t):
-        xf[t] = vis_ref[pl.ds(t * 32, 32), :].astype(f32)
+        for j in range(4):
+            xf[4 * t + j] = vis_ref[pl.ds(t * 128 + j * 32, 32), :].astype(f32)
 
     copy.wait()
     step = 32
@@ -102,11 +103,13 @@
                 packed[pl.ds(two & 0xFFFF, 1), :] = xf[at, pl.ds(j, 1), :]
                 packed[pl.ds(two >> 16, 1), :] = xf[at + BLK // (2 * step), pl.ds(j, 1), :]
 
-    @pl.loop(0, tiles)
-    def _(t):
-        rows_t = packed[pl.ds(t * CAP, CAP), :]
-        meta_t = jnp.broadcast_to(meta[pl.ds(t, 1), :], (SENT - CAP, FEAT))
-        out_ref[t] = jnp.concatenate([rows_t, meta_t], 0).astype(bf16)
+    @pl.loop(0, tiles // 4)
+    def _(group):
+        for j in range(4):
+            t = 4 * group + j
+            rows_t = packed[pl.ds(t * CAP, CAP), :]
+            meta_t = jnp.broadcast_to(meta[pl.ds(t, 1), :], (SENT - CAP, FEAT))
+            out_ref[t] = jnp.concatenate([rows_t, meta_t], 0).astype(bf16)
 
 
 def pack(visibility, destination, cell_u, cell_v, tap_u, tap_v, tiles):
@@ -131,9 +134,9 @@
 
 
 def grid_kernel(
-    recv_ref, table_hbm, out_hbm, ve_low, ve_high, ue_ref,
-    xf, xm, xs, ms, meta, meta_t, pos_v, pos_s, span_v, span_s,
-    wu_a, wu_b, taps_a, taps_b, xt_a, xt_b, wv_a, wv_b, table_ref, grid3, sems, out_sems,
+    recv_ref, table_hbm, grid3, ve_low, ve_high, ue_ref,
+    xf, xs, fields_ref, meta, meta_t, pos_v, pos_s, span_v, span_s,
+    wu_a, wu_b, taps_a, taps_b, xt_a, xt_b, wv_a, wv_b, table_ref, sems, out_sems,
 ):
     grid = grid3.reshape(EV * EU, FEAT)
     sources = recv_ref.shape[0]
@@ -141,11 +144,13 @@
     blocks = slots // BLK
     lanes = BLK // sources
 
-    @pl.loop(0, sources)
-    def _(s):
-        x = recv_ref[s].astype(f32)
-        xf[s] = x[:CAP]
-        meta[pl.ds(s, 1), :] = x[CAP:CAP + 1]
+    @pl.loop(0, sources // 4)
+    def _(t):
+        for j in range(4):
+            s = 4 * t + j
+            x = recv_ref[s].astype(f32)
+            xf[s] = x[:CAP]
+            meta[pl.ds(s, 1), :] = x[CAP:CAP + 1]
 
     table_copy = pltpu.make_async_copy(table_hbm, table_ref, sems.at[2])
     table_copy.start()
@@ -153,13 +158,15 @@
     meta_t[...] = placed.T
     keys = 64
 
+    def field_row(f, b):
+        return jnp.concatenate(
+            [meta_t[pl.ds(f * CAP + k, 1), :] for k in range(b * lanes, (b + 1) * lanes)], 1
+        )
+
     def key_row(b):
-        out = []
-        for k in range(b * lanes, (b + 1) * lanes):
-            cu1 = meta_t[pl.ds(k, 1), :].astype(i32)
-            cv1 = meta_t[pl.ds(CAP + k, 1), :].astype(i32)
-            out.append(jnp.where(cu1 > 0, (cv1 - 1) >> 1, keys))
-        return jnp.concatenate(out, 1)
+        cu1 = field_row(0, b).astype(i32)
+        cv1 = field_row(1, b).astype(i32)
+        return jnp.where(cu1 > 0, (cv1 - 1) >> 1, keys)
 
     key_ids = iota((128, BLK), 0)
     total = jnp.zeros((128, BLK), f32)
@@ -180,16 +187,25 @@
     span_copy.start()
     before = earlier(BLK)
     base = start[:, 0:1]
+    pos_rows = []
     for b in range(blocks):
         mine = (key_ids == key_row(b)).astype(f32)
         pos = jnp.sum(mine * (dot(mine.astype(bf16), before) + base), 0, keepdims=True)
         pos = pos.astype(i32)
+        pos_rows.append(pos)
         pos_v[pl.ds(b, 1), :] = pos[:, :BLK // 2] + (pos[:, BLK // 2:] << 16)
         base = base + jnp.sum(mine, 1, keepdims=True)
     pos_copy = pltpu.make_async_copy(pos_v, pos_s, sems.at[1])
     pos_copy.start()
-    for k in range(CAP):
-        xm[pl.ds(k * sources, sources), :] = pltpu.roll(placed, (FEAT - k) % FEAT, 1)
+    ordered = jnp.zeros((4 * blocks, BLK), f32)
+    chunk_ids = iota((blocks, BLK), 0)
+    place_ids = iota((BLK, BLK), 0)
+    for b in range(blocks):
+        chunk = chunk_ids == (pos_rows[b] >> 8)
+        values = jnp.concatenate([jnp.where(chunk, field_row(f, b), 0.0) for f in range(4)], 0)
+        place = (place_ids == (pos_rows[b] & (BLK - 1))).astype(f32).astype(bf16)
+        ordered = ordered + lax.dot_general(values.astype(bf16), place, NT, preferred_element_type=f32)
+    fields_ref[...] = ordered.astype(i32) - 1
 
     @pl.loop(0, EV)
     def _(t):
@@ -205,10 +221,8 @@
             two = pos_s[b, s]
             for k, p in ((2 * b, two & 0xFFFF), (2 * b + 1, two >> 16)):
                 xs[pl.ds(p, 1), :] = xf[s, pl.ds(k, 1), :]
-                ms[pl.ds(p, 1), :] = xm[pl.ds(k * sources + s, 1), :]
 
     table_tr = table_ref[...]
-    pick = (iota((8, FEAT), 1) == CAP * iota((8, FEAT), 0)).astype(f32).astype(bf16)
     phase_ids = iota((128, BLK), 0)
     u_ids = iota((EU, BLK), 0)
     t_ids = iota((GROUP + 4, BLK), 0)
@@ -226,8 +240,7 @@
         wu, taps, xt, wv = into
         part = pl.ds(c * BLK, BLK)
         xt[...] = xs[part, :].T.astype(bf16)
-        fields = lax.dot_general(pick, ms[part, :].astype(bf16), NT, preferred_element_type=f32).astype(i32) - 1
-        cu, cv, tu, tv = (fields[i:i + 1] for i in range(4))
+        cu, cv, tu, tv = (fields_ref[pl.ds(f * blocks + c, 1), :] for f in range(4))
         ku = dot(table_tr, (phase_ids == tu).astype(f32).astype(bf16))
         kv = dot(table_tr, (phase_ids == tv).astype(f32).astype(bf16))
         off = u_ids - (cu + 4)
@@ -264,13 +277,6 @@
                 v_at = v_first + g * GROUP
                 add_cells(v_at, wu, xt, v_weights(taps[...], v_at))
 
-    def out_copy(u):
-        return pltpu.make_async_copy(grid3.at[pl.ds(PAD, TV), 8 + u], out_hbm.at[u], out_sems.at[0])
-
-    @pl.loop(0, TU)
-    def _(u):
-        out_copy(u).start()
-
     ve_low[...] = grid[pl.ds(0, PAD * EU), :].astype(bf16)
     ve_high[...] = grid[pl.ds((TV + PAD) * EU, PAD * EU), :].astype(bf16)
 
@@ -284,10 +290,6 @@
     for e in range(2):
         for u in range(PAD):
             edge_copy(e, u).wait()
-
-    @pl.loop(0, TU)
-    def _(u):
-        out_copy(u).wait()
 
 
 def grid_rows(recv, table):
@@ -297,9 +299,9 @@
     return pl.pallas_call(
         grid_kernel,
         in_specs=[vmem, pl.BlockSpec(memory_space=pltpu.HBM)],
-        out_specs=(pl.BlockSpec(memory_space=pltpu.HBM), vmem, vmem, vmem),
+        out_specs=(vmem, vmem, vmem, vmem),
         out_shape=(
-            jax.ShapeDtypeStruct((TU, TV, FEAT), f32),
+            jax.ShapeDtypeStruct((EV, EU, FEAT), f32),
             jax.ShapeDtypeStruct((PAD * EU, FEAT), bf16),
             jax.ShapeDtypeStruct((PAD * EU, FEAT), bf16),
             jax.ShapeDtypeStruct((2, PAD, TV, FEAT), f32),
@@ -307,8 +309,7 @@
         scratch_shapes=[
             pltpu.VMEM((sources, CAP, FEAT), f32),
             pltpu.VMEM((slots, FEAT), f32),
-            pltpu.VMEM((slots, FEAT), f32),
-            pltpu.VMEM((slots, FEAT), f32),
+            pltpu.VMEM((4 * slots // BLK, BLK), i32),
             pltpu.VMEM((sources, FEAT), f32),
             pltpu.VMEM((FEAT, sources), f32),
             pltpu.VMEM((slots // BLK, BLK // 2), i32),
@@ -324,11 +325,10 @@
             pltpu.VMEM((GROUP + 4, BLK), bf16),
             pltpu.VMEM((GROUP + 4, BLK), bf16),
             pltpu.VMEM((TAPS, 128), bf16),
-            pltpu.VMEM((EV, EU, FEAT), f32),
             pltpu.SemaphoreType.DMA((3,)),
             pltpu.SemaphoreType.DMA((2,)),
         ],
-        compiler_params=pltpu.CompilerParams(vmem_limit_bytes=48 * MIB),
+        compiler_params=pltpu.CompilerParams(vmem_limit_bytes=24 * MIB),
         name="grid_rows",
     )(recv, table)
 
@@ -360,59 +360,50 @@
     )(low, high, ue)
 
 
-def v_edge_kernel(out_in, low_ref, high_ref, out_hbm, own_ref, low, high, edges, sems):
-    def copy(e, back):
-        there = out_hbm.at[:, pl.ds(e * (TV - 8), 8)]
-        ends = (edges.at[e], there) if back else (there, edges.at[e])
-        return pltpu.make_async_copy(*ends, sems.at[e])
-
-    copy(0, False).start()
-    copy(1, False).start()
-    low[...] = low_ref[...].astype(f32)
-    high[...] = high_ref[...].astype(f32)
-    for e, (halo, at) in enumerate(((low, 0), (high, 8 - PAD))):
-        copy(e, False).wait()
-
-        @pl.loop(0, TU // 8)
-        def _(t):
-            for j in range(8):
-                u = t * 8 + j
-                edges[e, u, at:at + PAD, :] += halo[pl.ds(8 + u, PAD, stride=EU), :]
-
-        copy(e, True).start()
-    copy(0, True).wait()
-    copy(1, True).wait()
-    own = [
-        pltpu.make_async_copy(out_hbm.at[pl.ds(e * (TU - PAD), PAD)], own_ref.at[e], sems.at[e])
-        for e in range(2)
-    ]
-    own[0].start()
-    own[1].start()
-    own[0].wait()
-    own[1].wait()
-
-
-def add_v_edges(out, low, high):
+def tile_kernel(grid_in, low_ref, high_ref, grid3, out_hbm, own_ref, sems):
+    for at, halo in ((PAD, low_ref), (TV, high_ref)):
+        for v in range(PAD):
+            grid3[at + v] += halo[pl.ds(v * EU, EU), :].astype(f32)
+
+    def out_copy(u):
+        return pltpu.make_async_copy(grid3.at[pl.ds(PAD, TV), 8 + u], out_hbm.at[u], sems.at[0])
+
+    def own_copy(e, u):
+        at = 8 + e * (TU - PAD) + u
+        return pltpu.make_async_copy(grid3.at[pl.ds(PAD, TV), at], own_ref.at[e, u], sems.at[1])
+
+    ends = [own_copy(e, u) for e in range(2) for u in range(PAD)]
+    for copy in ends:
+        copy.start()
+
+    @pl.loop(PAD, TU - PAD)
+    def _(u):
+        out_copy(u).start()
+
+    for copy in ends:
+        copy.wait()
+
+    @pl.loop(PAD, TU - PAD)
+    def _(u):
+        out_copy(u).wait()
+
+
+def write_tile(grid, low, high):
     vmem = pl.BlockSpec(memory_space=pltpu.VMEM)
-    hbm = pl.BlockSpec(memory_space=pl.ANY)
     return pl.pallas_call(
-        v_edge_kernel,
-        in_specs=[hbm, vmem, vmem],
-        out_specs=(hbm, vmem),
+        tile_kernel,
+        in_specs=[vmem] * 3,
+        out_specs=(vmem, pl.BlockSpec(memory_space=pltpu.HBM), vmem),
         out_shape=(
-            jax.ShapeDtypeStruct(out.shape, f32),
+            jax.ShapeDtypeStruct(grid.shape, f32),
+            jax.ShapeDtypeStruct((TU, TV, FEAT), f32),
             jax.ShapeDtypeStruct((2, PAD, TV, FEAT), f32),
         ),
-        scratch_shapes=[
-            pltpu.VMEM(low.shape, f32),
-            pltpu.VMEM(high.shape, f32),
-            pltpu.VMEM((2, TU, 8, FEAT), f32),
-            pltpu.SemaphoreType.DMA((2,)),
-        ],
+        scratch_shapes=[pltpu.SemaphoreType.DMA((2,))],
         input_output_aliases={0: 0},
-        compiler_params=pltpu.CompilerParams(vmem_limit_bytes=8 * MIB),
-        name="add_v_edges",
-    )(out, low, high)
+        compiler_params=pltpu.CompilerParams(vmem_limit_bytes=4 * MIB),
+        name="write_tile",
+    )(grid, low, high)
 
 
 def u_edge_kernel(out_in, low_ref, high_ref, own_ref, out_hbm, edges, sems):
@@ -453,13 +444,13 @@
     tiles = lax.axis_size("au") * lax.axis_size("vert")
     sent = pack(visibility, destination, cell_u, cell_v, tap_u, tap_v, tiles)
     recv = lax.all_to_all(sent, axes, split_axis=0, concat_axis=0, tiled=True)
-    out, ve_low, ve_high, ue = grid_rows(recv, kernel_table.T)
+    grid, ve_low, ve_high, ue = grid_rows(recv, kernel_table.T)
     v_low = shifted(ve_high, "vert", True)
     v_high = shifted(ve_low, "vert", False)
     send_low, send_high = add_corners(v_low, v_high, ue)
     u_low = shifted(send_high, "au", True)
     u_high = shifted(send_low, "au", False)
-    out, own = add_v_edges(out, v_low, v_high)
+    _, out, own = write_tile(grid, v_low, v_high)
     return add_u_edges(out, u_low, u_high, own)
 
 

time: 86.3 us -> 78 us (0.904)
  the two profiles are of different devices: /device:TPU:1 before, /device:TPU:3 now
where the time goes in v1:
time: 78 us; the launch traced here: 77.6 us
  blocking collectives  31.9 us (41%)
  Pallas kernels  26 us (33%)
  starting transfers between devices  14.9 us (19%)
  waiting for transfers between devices  4.05 us (5%)
    all_to_all x1, blocking collectives, local(): recv = lax.all_to_all(sent, axes, split_axis=0, concat_axis=0, tiled=True)  31.9 us
    pallas_call x1, Pallas kernels, grid_rows(): pl.pallas_call(grid_kernel, in_specs=[vmem, pl.BlockSpec(memory_space=plt...  15.4 us
    ppermute x4, starting transfers between devices, shifted(): return lax.ppermute(x, axis, pairs)  14.9 us
    pallas_call x1, Pallas kernels, pack(): pl.pallas_call(pack_kernel, in_specs=[pl.BlockSpec(memory_space=pltpu.HBM...  6.21 us
    ppermute x4, waiting for transfers between devices, shifted(): return lax.ppermute(x, axis, pairs)  4.05 us
    pallas_call x1, Pallas kernels, write_tile(): pl.pallas_call(tile_kernel, in_specs=[vmem] * 3, out_specs=(vmem, pl.Bloc...  3.48 us
  transfers between devices with their start and end apart: 4, of which 1 were waited for; matrix products, arithmetic and copies ran while one was open for 0% of the time, Pallas kernels for 4%

profile of v1, /device:TPU:3, one launch (start us, length us, event | category | flops | bytes accessed | tf_op | source)
XLA Modules:
  0.0 77.6 jit_solution(9357096642950599403)
XLA Ops:
  0.0 6.2 %pack_rows.1 = bf16[128,40,128]{2,1,0:T(8,128)(2,1)} custom-call(s32[1,2048]{1,0:T(1,128)} %bitcast.7, s32[1,2048]{1,0:T(1,128)} %bitcast.8, s32[1,2048]{1,0:T(1,128)} %bitcast.9, s32[1,2048]{1,0:T(1,128)} %bitcast.10, s32[1,2048]{1,0:T(1,128)} %bitcast.11, bf16[2048,128]{1,0:T(8,128)(2,1)} %vis_hbm.1), custom_call_target="tpu_custom_call" | custom-call | tf_op jit(solution)/shard_map/pack_rows/pallas_call | solution.py:118
  6.2 31.9 %all_to_all.5.recv_ref = bf16[128,40,128]{2,1,0:T(8,128)(2,1)S(1)} all-to-all(bf16[128,40,128]{2,1,0:T(8,128)(2,1)} %pack_rows.1), channel_id=1, replica_groups=mesh['au'=16,'vert'=8] {'au','vert'}, dimensions={0} | all-to-all | bytes 2621440 | tf_op jit(solution)/shard_map/all_to_all | solution.py:446
  38.1 0.0 copy-start
  38.1 0.7 copy-done
  38.8 15.4 %grid_rows.1 = (f32[160,144,128]{2,1,0:T(8,128)S(1)}, bf16[576,128]{1,0:T(8,128)(2,1)S(1)}, bf16[576,128]{1,0:T(8,128)(2,1)S(1)}, f32[2,4,128,128]{3,2,1,0:T(8,128)S(1)}) custom-call(bf16[128,40,128]{2,1,0:T(8,128)(2,1)S(1)} %all_to_all.5.recv_ref, bf16[8,128]{1,0:T(8,128)(2,1)S(1)} %bitcast.6), custom_call_target="tpu_custom_call" | custom-call | tf_op jit(solution)/shard_map/grid_rows/pallas_call | solution.py:299
  54.2 2.0 %collective-permute-start = (bf16[576,128]{1,0:T(8,128)(2,1)S(1)}, bf16[576,128]{1,0:T(8,128)(2,1)S(1)}, u32[]{:S(2)}, u32[]{:S(2)}) collective-permute-start(bf16[576,128]{1,0:T(8,128)(2,1)S(1)} %get-tuple-element.14), channel_id=1, source_target_pairs={{0,1},{1,2},{2,3},{3,4},{4,5},{5,6},{6,7},{8,9},{9,10},{10,11},{11... | collective-permute-start | bytes 442376 | tf_op jit(solution)/shard_map/ppermute | solution.py:439
  56.1 2.4 %collective-permute-start.1 = (bf16[576,128]{1,0:T(8,128)(2,1)S(1)}, bf16[576,128]{1,0:T(8,128)(2,1)S(1)}, u32[]{:S(2)}, u32[]{:S(2)}) collective-permute-start(bf16[576,128]{1,0:T(8,128)(2,1)S(1)} %get-tuple-element.15), channel_id=1, source_target_pairs={{1,0},{2,1},{3,2},{4,3},{5,4},{6,5},{7,6},{9,8},{10,9},{11,10},{12... | collective-permute-start | bytes 442376 | tf_op jit(solution)/shard_map/ppermute | solution.py:439
  58.6 0.0 collective-permute-done.low_ref
  58.6 4.0 %collective-permute-done.1.high_ref = bf16[576,128]{1,0:T(8,128)(2,1)S(1)} collective-permute-done((bf16[576,128]{1,0:T(8,128)(2,1)S(1)}, bf16[576,128]{1,0:T(8,128)(2,1)S(1)}, u32[]{:S(2)}, u32[]{:S(2)}) %collective-permute-start.1) | collective-permute-done | bytes 147488 | tf_op jit(solution)/shard_map/ppermute | solution.py:439
  62.6 0.1 add_corners.1
  62.7 5.4 %collective-permute-start.2 = (bf16[4,128,128]{2,1,0:T(8,128)(2,1)S(1)}, bf16[4,128,128]{2,1,0:T(8,128)(2,1)S(1)}, u32[]{:S(2)}, u32[]{:S(2)}) collective-permute-start(bf16[4,128,128]{2,1,0:T(8,128)(2,1)S(1)} %get-tuple-element.18), channel_id=1, source_target_pairs={{0,8},{8,16},{16,24},{24,32},{32,40},{40,48},{48,56},{56,64},{64,7... | collective-permute-start | bytes 393224 | tf_op jit(solution)/shard_map/ppermute | solution.py:439
  68.1 5.2 %collective-permute-start.3 = (bf16[4,128,128]{2,1,0:T(8,128)(2,1)S(1)}, bf16[4,128,128]{2,1,0:T(8,128)(2,1)S(1)}, u32[]{:S(2)}, u32[]{:S(2)}) collective-permute-start(bf16[4,128,128]{2,1,0:T(8,128)(2,1)S(1)} %get-tuple-element.19), channel_id=1, source_target_pairs={{8,0},{16,8},{24,16},{32,24},{40,32},{48,40},{56,48},{64,56},{72,6... | collective-permute-start | bytes 393224 | tf_op jit(solution)/shard_map/ppermute | solution.py:439
  73.3 3.5 %write_tile.1 = (f32[160,144,128]{2,1,0:T(8,128)S(1)}, f32[128,128,128]{2,1,0:T(8,128)}, f32[2,4,128,128]{3,2,1,0:T(8,128)S(1)}) custom-call(f32[160,144,128]{2,1,0:T(8,128)S(1)} %get-tuple-element.13.grid_in, bf16[576,128]{1,0:T(8,128)(2,1)S(1)} %collective-permute-done.low_ref, ...), custom_call_target="tpu_custom_call", output_to_operand_aliasing={{0}: (0, {})} | custom-call | tf_op jit(solution)/shard_map/write_tile/pallas_call | solution.py:393
  76.8 0.0 collective-permute-done.2.low_ref
  76.8 0.0 collective-permute-done.3.high_ref
  76.8 0.8 %add_u_edges.1 = f32[128,128,128]{2,1,0:T(8,128)} custom-call(f32[128,128,128]{2,1,0:T(8,128)} %get-tuple-element.16.out_in, bf16[4,128,128]{2,1,0:T(8,128)(2,1)S(1)} %collective-permute-done.2.low_ref, bf16[4,128,128]{2,1,0:T(8,128)(2,1)S(1)} %collective-permute-done.3.high_ref, ...), custom_call_target="tpu_custom_call", output_to_operand_aliasing={{}: (0, {})} | custom-call | tf_op jit(solution)/shard_map/add_u_edges/pallas_call | solution.py:424
Async XLA Ops:
  38.1 0.7 copy-start
  54.2 4.4 %collective-permute-start = (bf16[576,128]{1,0:T(8,128)(2,1)S(1)}, bf16[576,128]{1,0:T(8,128)(2,1)S(1)}, u32[]{:S(2)}, u32[]{:S(2)}) collective-permute-start(bf16[576,128]{1,0:T(8,128)(2,1)S(1)} %get-tuple-element.14), channel_id=1, source_target_pairs={{0,1},{1,2},{2,3},{3,4},{4,5},{5,6},{6,7},{8,9},{9,10},{10,11},{11... | collective-permute-start | bytes 442376 | tf_op jit(solution)/shard_map/ppermute | solution.py:439
  56.1 6.5 %collective-permute-start.1 = (bf16[576,128]{1,0:T(8,128)(2,1)S(1)}, bf16[576,128]{1,0:T(8,128)(2,1)S(1)}, u32[]{:S(2)}, u32[]{:S(2)}) collective-permute-start(bf16[576,128]{1,0:T(8,128)(2,1)S(1)} %get-tuple-element.15), channel_id=1, source_target_pairs={{1,0},{2,1},{3,2},{4,3},{5,4},{6,5},{7,6},{9,8},{10,9},{11,10},{12... | collective-permute-start | bytes 442376 | tf_op jit(solution)/shard_map/ppermute | solution.py:439
  62.7 14.1 %collective-permute-start.2 = (bf16[4,128,128]{2,1,0:T(8,128)(2,1)S(1)}, bf16[4,128,128]{2,1,0:T(8,128)(2,1)S(1)}, u32[]{:S(2)}, u32[]{:S(2)}) collective-permute-start(bf16[4,128,128]{2,1,0:T(8,128)(2,1)S(1)} %get-tuple-element.18), channel_id=1, source_target_pairs={{0,8},{8,16},{16,24},{24,32},{32,40},{40,48},{48,56},{56,64},{64,7... | collective-permute-start | bytes 393224 | tf_op jit(solution)/shard_map/ppermute | solution.py:439
  68.1 8.7 %collective-permute-start.3 = (bf16[4,128,128]{2,1,0:T(8,128)(2,1)S(1)}, bf16[4,128,128]{2,1,0:T(8,128)(2,1)S(1)}, u32[]{:S(2)}, u32[]{:S(2)}) collective-permute-start(bf16[4,128,128]{2,1,0:T(8,128)(2,1)S(1)} %get-tuple-element.19), channel_id=1, source_target_pairs={{8,0},{16,8},{24,16},{32,24},{40,32},{48,40},{56,48},{64,56},{72,6... | collective-permute-start | bytes 393224 | tf_op jit(solution)/shard_map/ppermute | solution.py:439
